TPU v7x, 32 devices: a whole 2x2x4 slice. The times are simulated.
32 devices in a mesh: groups: 2 (over y), ep: 8 (over z, core), tp: 2 (over x).
Axes of the slice: x: 2, y: 2, z: 4, core: 2. Of those that a mesh axis runs over, the one named last changes fastest.
Arguments:
- queries: bfloat16 [1024, 4096], P(('groups', 'ep', 'tp')), parts along dimension 0, may hold values from -6 to 6
- new_kv: bfloat16 [1024, 4, 256], P(('groups', 'ep', 'tp')), parts along dimension 0, may hold values from -6 to 6
- cache: bfloat16 [1024, 4, 32, 256], P(('groups', 'ep', 'tp')), parts along dimension 0, may hold values from -6 to 6
- lengths: int32 [1024], P(('groups', 'ep', 'tp')), parts along dimension 0, may hold values from 2 to 32, as said below
- out_weight: bfloat16 [4096, 2048], P('tp'), may hold values from -0.09375 to 0.09375
- residual: bfloat16 [1024, 2048], P(('groups', 'ep'), 'tp'), parts along dimension 0, may hold values from -10 to 10
- norm_gain: float32 [2048], replicated, may hold values from 0.25 to 1.75
- expert_ids: int32 [1024, 8], P(('groups', 'ep')), parts along dimension 0, may hold values from 0 to 15, all different within a row; in each aligned block of 64 rows (0 to 63, 64 to 127, ...) at most 64 rows name the same one
- expert_gates: float32 [1024, 8], P(('groups', 'ep')), parts along dimension 0, may hold values from 0.05 to 1
- w_gate: bfloat16 [2048, 12288], P(None, ('ep', 'tp')), may hold values from -0.125 to 0.125
- w_up: bfloat16 [2048, 12288], P(None, ('ep', 'tp')), may hold values from -0.125 to 0.125
- w_down: bfloat16 [12288, 2048], P(('ep', 'tp')), may hold values from -0.21875 to 0.21875
Outputs:
- layer_out: bfloat16 [1024, 2048], P(('groups', 'ep'), 'tp'), parts along dimension 0
There are 2 independent parts, one for each index of `groups`. A program takes and returns all parts, laid end to end along the dimension named above; an argument that names none is the same for every part. Nothing has to cross between parts.
Inputs may be any that keep to these rules, and one draw needn't show every extreme that they name: `expert_ids`: each row names 8 different experts; in the 64 rows of one index of ep (aligned blocks of rows) no expert is named by more than 64 rows, a bound that some block reaches. `lengths`: some row has the full 32 positions.
All inputs are finite; a program needn't handle non-finite values.
Results may differ from a plain program's by a relative error of at most 0.009.
Values may be sent and summed in bfloat16 or wider, within the bound.
A program may use at most 128 MiB of HBM per device.

v0:
```python
import math

import jax
import jax.numpy as jnp
from jax import lax
from jax.sharding import PartitionSpec as P

D = 2048
TOPK = 8
EXP_DEV = 2


epsilon = 1e-06


def attend(queries, new_kv, cache, lengths):
    row_count = queries.shape[0]
    kv_local = cache.shape[1]
    positions = cache.shape[2]
    head_dim = cache.shape[3] // 2
    group_size = queries.shape[1] // (head_dim * kv_local)
    query = queries.reshape(row_count, kv_local, group_size, head_dim)
    key_part = cache[..., :head_dim]
    value_part = cache[..., head_dim:]
    score_scale = 1.0 / math.sqrt(head_dim)
    scores = (
        jnp.einsum("rgqd,rgcd->rgqc", query, key_part, preferred_element_type=jnp.float32)
        * score_scale
    )
    fresh_score = (
        jnp.einsum(
            "rgqd,rgd->rgq", query, new_kv[..., :head_dim], preferred_element_type=jnp.float32
        )
        * score_scale
    )
    is_valid = (jnp.arange(positions, dtype=jnp.int32)[None, :] < lengths[:, None])[
        :, None, None, :
    ]
    masked = jnp.where(is_valid, scores, -1e30)
    row_max = jnp.maximum(jnp.max(masked, -1), fresh_score)
    exp_terms = jnp.where(is_valid, jnp.exp(masked - row_max[..., None]), 0.0)
    fresh_exp = jnp.exp(fresh_score - row_max)
    totals = jnp.sum(exp_terms, -1) + fresh_exp
    weights = (exp_terms / totals[..., None]).astype(jnp.bfloat16)
    fresh_weight = (fresh_exp / totals).astype(jnp.bfloat16)
    mixed = jnp.einsum("rgqc,rgcd->rgqd", weights, value_part, preferred_element_type=jnp.float32)
    mixed = mixed + fresh_weight.astype(jnp.float32)[..., None] * new_kv[
        :, :, None, head_dim:
    ].astype(jnp.float32)
    return mixed.astype(jnp.bfloat16).reshape(row_count, kv_local * group_size * head_dim)


def slot_tables(expert_ids, expert_gates, experts, capacity):
    route_weights = expert_gates / jnp.sum(expert_gates, 1, keepdims=True)
    matches = expert_ids[:, :, None] == jnp.arange(experts, dtype=jnp.int32)[None, None, :]
    chosen = jnp.any(matches, 1)
    slot_rank = jnp.cumsum(chosen.astype(jnp.int32), 0) - 1
    slot_map = chosen[None] & (
        slot_rank[None] == jnp.arange(capacity, dtype=jnp.int32)[:, None, None]
    )
    return (slot_map, slot_rank, route_weights)


def run_expert(gathered, w_gate, w_up, w_down):
    gate_proj = jnp.einsum("qcd,df->qcf", gathered, w_gate, preferred_element_type=jnp.float32)
    up_proj = jnp.einsum("qcd,df->qcf", gathered, w_up, preferred_element_type=jnp.float32)
    activated = (jax.nn.silu(gate_proj) * up_proj).astype(jnp.bfloat16)
    projected = jnp.einsum("qcf,fd->qcd", activated, w_down, preferred_element_type=jnp.float32)
    return lax.all_to_all(
        projected.astype(jnp.bfloat16), "ep", split_axis=0, concat_axis=0, tiled=True
    ).astype(projected.dtype)


def per_device(
    queries,
    new_kv,
    cache,
    lengths,
    out_weight,
    residual,
    norm_gain,
    expert_ids,
    expert_gates,
    w_gate,
    w_up,
    w_down,
):
    row_count = residual.shape[0]
    col_width = residual.shape[1]
    ep_size = lax.axis_size("ep")
    tp_size = lax.axis_size("tp")
    tp_rank = lax.axis_index("tp")
    experts = ep_size * EXP_DEV
    capacity = min(row_count, 2 * row_count * TOPK // experts)
    pieces = tp_size // EXP_DEV
    parity = tp_rank // pieces
    attn_local = attend(queries, new_kv, cache, lengths)
    attn_heads = lax.all_to_all(attn_local, "tp", split_axis=1, concat_axis=0, tiled=True)
    partial_value = jnp.dot(attn_heads, out_weight, preferred_element_type=jnp.float32)
    normed_full = None
    normed_share = None
    head_share = lax.psum_scatter(partial_value, "tp", scatter_dimension=1, tiled=True)
    hidden_share = (residual.astype(jnp.float32) + head_share).astype(jnp.bfloat16)
    hidden_f = hidden_share.astype(jnp.float32)
    squares = lax.psum(jnp.sum(hidden_f * hidden_f, 1, keepdims=True), "tp")
    inv_scale = lax.rsqrt(squares / D + epsilon)
    gain_share = lax.dynamic_slice_in_dim(norm_gain, tp_rank * col_width, col_width)
    normed_share = (hidden_f * inv_scale * gain_share).astype(jnp.bfloat16)
    slot_map, slot_rank, route_weights = slot_tables(expert_ids, expert_gates, experts, capacity)
    slot_grid = slot_map.reshape(capacity, row_count, ep_size, EXP_DEV)
    own_slots = lax.dynamic_index_in_dim(slot_grid, parity, 3, keepdims=False)
    normed_full = lax.all_gather(normed_share, "tp", axis=1, tiled=True)
    outgoing = jnp.einsum(
        "crq,rd->qcd",
        own_slots.astype(jnp.bfloat16),
        normed_full,
        preferred_element_type=jnp.float32,
    ).astype(jnp.bfloat16)
    returned = run_expert(
        lax.all_to_all(outgoing, "ep", split_axis=0, concat_axis=0, tiled=True),
        w_gate,
        w_up,
        w_down,
    )
    picked_rank = jnp.take_along_axis(slot_rank, expert_ids, 1)
    owner = expert_ids // EXP_DEV
    member = expert_ids % EXP_DEV
    flat = returned.reshape(ep_size * capacity, returned.shape[-1])
    index = owner * capacity + picked_rank
    weight = jnp.where(member == parity, route_weights, 0.0)
    moe_part = jnp.sum(weight[:, :, None] * flat[index], 1)
    moe_share = lax.psum_scatter(
        moe_part.astype(jnp.bfloat16), "tp", scatter_dimension=1, tiled=True
    ).astype(jnp.float32)
    return (hidden_share.astype(jnp.float32) + moe_share).astype(jnp.bfloat16)


def solution(mesh):
    in_specs = (
        P(("groups", "ep", "tp"), None),
        P(("groups", "ep", "tp"), None, None),
        P(("groups", "ep", "tp"), None, None, None),
        P(("groups", "ep", "tp")),
        P("tp", None),
        P(("groups", "ep"), "tp"),
        P(),
        P(("groups", "ep"), None),
        P(("groups", "ep"), None),
        P(None, ("ep", "tp")),
        P(None, ("ep", "tp")),
        P(("ep", "tp"), None),
    )
    out_specs = P(("groups", "ep"), "tp")
    return jax.shard_map(
        per_device, mesh=mesh, in_specs=in_specs, out_specs=out_specs, check_vma=False
    )
```

profile of v0, /device:TPU:0, one launch (start us, length us, event | category | flops | bytes accessed | tf_op | source)
XLA Modules:
  0.0 211.0 jit_solution(17930872633224698782)
XLA Ops:
  6.5 0.0 copy-start
  6.5 0.0 reduce-scatter.3.cloned.1.call-start
  6.5 0.9 iota_compare_fusion.2
  7.4 0.0 copy-start.2
  7.4 1.1 copy.57
  8.6 0.8 slice_bitcast_fusion
  9.4 0.3 fusion.34
  9.6 2.0 fusion.46
  11.7 0.4 fusion.19
  12.1 0.1 fusion.38
  12.2 0.0 copy-done.2
  12.2 1.2 fusion.14
  13.4 1.0 all_to_all.20
  14.4 0.1 copy.46
  14.5 9.2 %all_to_all.29 = bf16[32,2,2048]{2,0,1:T(8,128)(2,1)S(1)} all-to-all(bf16[32,2,2048]{2,0,1:T(8,128)(2,1)S(1)} %copy.46), channel_id=1, replica_groups=mesh['groups'=2,'ep'=8,'tp'=2] {'tp'}, dimensions={1} | all-to-all | bytes 524288 | tf_op jit(solution)/shard_map/all_to_all | solution.py:98
  23.6 0.0 copy-start.4
  23.6 0.0 copy-start.6
  23.7 0.0 copy-start.3
  23.7 5.8 %fusion.47 = f32[64,2048]{1,0:T(8,128)} fusion(bf16[64,2048]{1,0:T(8,128)(2,1)S(1)} %bitcast.58, bf16[2048,2048]{1,0:T(8,128)(2,1)} %param.16), kind=kOutput, calls=%fused_computation.77 | convolution fusion | flops 536870912 | bytes 9175040 | tf_op jit(solution)/shard_map/dot_general | solution.py:99
  29.4 0.0 reduce-scatter.3.cloned.1.call-update
  29.5 0.0 copy-done.4
  29.5 0.1 copy.49
  29.6 0.1 reduce_window_sum.11
  29.7 0.1 copy.50
  29.8 0.0 copy-done.6
  29.9 14.7 %reduce-scatter.3.cloned.1.call-done = f32[64,1024]{1,0:T(8,128)} async-done(((f32[64,2048]{1,0:T(8,128)}), f32[64,1024]{1,0:T(8,128)}) %reduce-scatter.3.cloned.1.call-update) | async-done | bytes 262160 | tf_op jit(solution)/shard_map/reduce_scatter | solution.py:102
  44.6 0.0 copy-done.3
  44.6 1.1 fusion.20
  45.7 4.9 %psum.7 = f32[64,1]{0,1:T(1,128)S(1)} all-reduce(f32[64,1]{0,1:T(1,128)S(1)} %bitcast.65), channel_id=1, replica_groups=mesh['groups'=2,'ep'=8,'tp'=2] {'tp'}, use_global_device_ids=true, to_apply=%region_5.6 | all-reduce | flops 64 | bytes 512 | tf_op jit(solution)/shard_map/psum | solution.py:105
  50.6 0.1 fusion.22
  50.8 5.6 %all_gather.3 = bf16[64,2048]{1,0:T(8,128)(2,1)S(1)} all-gather(bf16[64,1024]{1,0:T(8,128)(2,1)S(1)} %fusion.22), channel_id=1, replica_groups=mesh['groups'=2,'ep'=8,'tp'=2] {'tp'}, dimensions={1}, use_global_device_ids=true | all-gather | bytes 393216 | tf_op jit(solution)/shard_map/all_gather | solution.py:112
  56.4 0.7 fusion.10
  57.1 0.0 copy-start.7
  57.1 53.7 %all_to_all.30 = bf16[8,64,2048]{2,1,0:T(8,128)(2,1)S(1)} all-to-all(bf16[8,64,2048]{2,1,0:T(8,128)(2,1)S(1)} %fusion.10), channel_id=1, replica_groups=mesh['groups'=2,'ep'=8,'tp'=2] {'ep'}, dimensions={0} | all-to-all | bytes 4194304 | tf_op jit(solution)/shard_map/all_to_all | solution.py:120
  110.8 0.0 copy-start.1
  110.8 1.3 copy-done.1
  112.1 0.0 copy-done.7
  112.1 3.0 %fusion.5 = f32[8,64,768]{2,1,0:T(8,128)} fusion(bf16[8,64,2048]{2,1,0:T(8,128)(2,1)S(1)} %all_to_all.30, bf16[2048,768]{1,0:T(8,128)(2,1)S(1)} %copy-done.7), kind=kOutput, calls=%fused_computation.8 | convolution fusion | flops 1610612736 | bytes 6815744 | tf_op jit(solution)/shard_map/qcd,df->qcf/dot_general | solution.py:65
  115.1 0.0 copy-done
  115.1 8.3 %fusion.7 = bf16[8,64,2048]{2,1,0:T(8,128)(2,1)} fusion(bf16[768,2048]{1,0:T(8,128)(2,1)S(1)} %copy-done, f32[8,64,768]{2,1,0:T(8,128)} %fusion.5, bf16[8,64,2048]{2,1,0:T(8,128)(2,1)} %copy-done.1, bf16[2048,768]{1,0:T(8,128)(2,1)} %param.22), kind=kOutput, calls=%fused_computation.10 | convolution fusion | flops 3224633344 | bytes 12058624 | tf_op jit(solution)/shard_map/qcf,fd->qcd/dot_general | solution.py:68
  123.4 4.3 %all-to-all-start.2 = ((bf16[8,64,2048]{2,1,0:T(8,128)(2,1)}), bf16[8,64,2048]{2,1,0:T(8,128)(2,1)}, u32[]{:S(2)}, u32[]{:S(2)}) async-start(bf16[8,64,2048]{2,1,0:T(8,128)(2,1)} %fusion.7), calls=%async_computation.3 | async-start | bytes 4194304 | tf_op jit(solution)/shard_map/all_to_all | solution.py:69
  127.7 0.2 reduce-scatter.5.cloned.1.call-start
  128.0 0.1 copy.52
  128.1 0.1 reshape.75
  128.2 0.0 copy-start.5
  128.2 3.8 %gather_fusion.1 = s32[512]{0:T(512)S(1)} fusion(s32[64,16]{1,0:T(8,128)S(1)} %broadcast_add_fusion, s32[512]{0:T(512)S(1)} %reshape.75), kind=kCustom, calls=%fused_computation.1 | custom fusion | bytes 8192 | tf_op jit(solution)/shard_map/jit(take_along_axis)/gather | solution.py:125
  131.9 0.1 reshape.78
  132.0 0.1 copy.53
  132.1 0.1 copy.54
  132.2 0.1 reshape.69
  132.3 0.0 copy-done.5
  132.4 0.1 copy.47
  132.4 44.4 %all-to-all-done.2 = bf16[8,64,2048]{2,1,0:T(8,128)(2,1)} async-done(((bf16[8,64,2048]{2,1,0:T(8,128)(2,1)}), bf16[8,64,2048]{2,1,0:T(8,128)(2,1)}, u32[]{:S(2)}, u32[]{:S(2)}) %all-to-all-start.2) | async-done | bytes 2097184 | tf_op jit(solution)/shard_map/all_to_all | solution.py:69
  176.8 4.0 %bitcast_convert_fusion = f32[512,2048]{1,0:T(8,128)} fusion(bf16[8,64,2048]{2,1,0:T(8,128)(2,1)} %all-to-all-done.2), kind=kLoop, calls=%fused_computation.13 | loop fusion | flops 1048576 | bytes 6291456 | tf_op jit(solution)/shard_map/reshape | solution.py:128
  180.8 7.6 %gather_fusion = f32[512,2048]{1,0:T(8,128)} fusion(f32[512,2048]{1,0:T(8,128)} %bitcast_convert_fusion, s32[1024]{0:T(1024)S(1)} %pad_clamp_fusion), kind=kCustom, calls=%fused_computation | custom fusion | bytes 8390656 | tf_op jit(solution)/shard_map/gather | solution.py:131
  188.5 4.3 %fusion = bf16[64,2048]{1,0:T(8,128)(2,1)} fusion(f32[512,2048]{1,0:T(8,128)} %gather_fusion, f32[64,8]{1,0:T(8,128)S(1)} %copy.47), kind=kLoop, calls=%fused_computation.3 | loop fusion | flops 1966080 | bytes 4458496 | tf_op jit(solution)/shard_map/reduce_sum | solution.py:131
  192.8 0.0 reduce-scatter.5.cloned.1.call-update
  192.8 9.7 %reduce-scatter.5.cloned.1.call-done = bf16[64,1024]{1,0:T(8,128)(2,1)} async-done(((bf16[64,2048]{1,0:T(8,128)(2,1)}), bf16[64,1024]{1,0:T(8,128)(2,1)}) %reduce-scatter.5.cloned.1.call-update) | async-done | bytes 131088 | tf_op jit(solution)/shard_map/reduce_scatter | solution.py:132
  202.6 1.6 fusion.23
  (16 shorter events, 0.2 us)
Async XLA Ops:
  6.5 108.6 %copy-start = (bf16[768,2048]{1,0:T(8,128)(2,1)S(1)}, bf16[768,2048]{1,0:T(8,128)(2,1)}, u32[]{:S(2)}) copy-start(bf16[768,2048]{1,0:T(8,128)(2,1)} %param.23) | copy-start | bytes 9437188
  6.5 38.1 %reduce-scatter.3.cloned.1.call-start = ((), (), s32[]{:S(2)}) async-start(), calls=%async_computation.5 | async-start | bytes 786432 | tf_op jit(solution)/shard_map/reduce_scatter | solution.py:102
  7.4 4.8 %copy-start.2 = (bf16[32,4,32,256]{3,2,1,0:T(8,128)(2,1)S(1)}, bf16[32,4,32,256]{3,2,1,0:T(8,128)(2,1)}, u32[]{:S(2)}) copy-start(bf16[32,4,32,256]{3,2,1,0:T(8,128)(2,1)} %param.14) | copy-start | bytes 6291460
  23.6 5.8 %copy-start.4 = (s32[64,8]{0,1:T(8,128)S(1)}, s32[64,8]{0,1:T(8,128)}, u32[]{:S(2)}) copy-start(s32[64,8]{0,1:T(8,128)} %param.19) | copy-start | bytes 6148
  23.6 6.2 %copy-start.6 = (f32[2048]{0:T(1024)S(1)}, f32[2048]{0:T(1024)}, u32[]{:S(2)}) copy-start(f32[2048]{0:T(1024)} %param.18) | copy-start | bytes 24580
  23.7 20.9 %copy-start.3 = (bf16[64,1024]{1,0:T(8,128)(2,1)S(1)}, bf16[64,1024]{1,0:T(8,128)(2,1)}, u32[]{:S(2)}) copy-start(bf16[64,1024]{1,0:T(8,128)(2,1)} %param.17) | copy-start | bytes 393220
  57.1 55.0 %copy-start.7 = (bf16[2048,768]{1,0:T(8,128)(2,1)S(1)}, bf16[2048,768]{1,0:T(8,128)(2,1)}, u32[]{:S(2)}) copy-start(bf16[2048,768]{1,0:T(8,128)(2,1)} %param.21) | copy-start | bytes 9437188
  110.8 1.3 copy-start.1
  123.4 53.4 %all-to-all-start.2 = ((bf16[8,64,2048]{2,1,0:T(8,128)(2,1)}), bf16[8,64,2048]{2,1,0:T(8,128)(2,1)}, u32[]{:S(2)}, u32[]{:S(2)}) async-start(bf16[8,64,2048]{2,1,0:T(8,128)(2,1)} %fusion.7), calls=%async_computation.3 | async-start | bytes 4194304 | tf_op jit(solution)/shard_map/all_to_all | solution.py:69
  127.7 74.8 %reduce-scatter.5.cloned.1.call-start = ((), (), s32[]{:S(2)}) async-start(), calls=%async_computation.6 | async-start | bytes 393216 | tf_op jit(solution)/shard_map/reduce_scatter | solution.py:132
  128.2 4.1 %copy-start.5 = (f32[64,8]{0,1:T(8,128)S(1)}, f32[64,8]{0,1:T(8,128)}, u32[]{:S(2)}) copy-start(f32[64,8]{0,1:T(8,128)} %param.20) | copy-start | bytes 6148
Sparse Core Ops, SparseCore 0:
  29.6 14.9 reduce-scatter.2
  193.0 9.5 reduce-scatter.4
where the time goes:
time: 211 us
  blocking collectives  73.5 us (35%)
  waiting for transfers between devices  68.8 us (33%)
  matrix products  21.2 us (10%)
  local copies, waits for them, and re-layouts  15.7 us (7%)
  other arithmetic  13.6 us (6%)
  between operations  13.6 us (6%)
  starting transfers between devices  4.56 us (2%)
    all_to_all x1, blocking collectives, per_device(): lax.all_to_all(outgoing, 'ep', split_axis=0, concat_axis=0, tiled=True)  53.7 us
    all_to_all x1, waiting for transfers between devices, run_expert(): lax.all_to_all(projected.astype(jnp.bfloat16), 'ep', split_axis=0, concat...  44.4 us
    reduce_scatter x1, waiting for transfers between devices, per_device(): lax.psum_scatter(partial_value, 'tp', scatter_dimension=1, tiled=True)  14.7 us
    reduce_scatter x1, waiting for transfers between devices, per_device(): lax.psum_scatter(moe_part.astype(jnp.bfloat16), 'tp', scatter_dimension=1...  9.73 us
    all_to_all x1, blocking collectives, per_device(): lax.all_to_all(attn_local, 'tp', split_axis=1, concat_axis=0, tiled=True)  9.18 us
    dot_general x1, matrix products, run_expert(): jnp.einsum('qcf,fd->qcd', activated, w_down, preferred_element_type=jnp.f...  8.28 us
    gather x1, local copies, waits for them, and re-layouts, per_device(): moe_part = jnp.sum(weight[:, :, None] * flat[index], 1)  7.61 us
    dot_general x1, matrix products, per_device(): jnp.dot(attn_heads, out_weight, preferred_element_type=jnp.float32)  5.79 us
  transfers between devices with their start and end apart: 3, of which 3 were waited for; matrix products, arithmetic and copies ran while one was open for 2% of the time, Pallas kernels for 0%

commit v1 on v0

--- a/solution.py
+++ b/solution.py
@@ -1,9 +1,16 @@
+import functools
 import math
 
 import jax
 import jax.numpy as jnp
 from jax import lax
+from jax.experimental import pallas as pl
+from jax.experimental.pallas import tpu as pltpu
 from jax.sharding import PartitionSpec as P
+
+MESH = pl.DeviceIdType.MESH
+CORES = 2
+TILE = 256
 
 D = 2048
 TOPK = 8
@@ -135,6 +142,493 @@
     return (hidden_share.astype(jnp.float32) + moe_share).astype(jnp.bfloat16)
 
 
+def layer_kernel(
+    ep_size,
+    kvh,
+    q_ref,
+    new_ref,
+    len_ref,
+    resid_ref,
+    gain_ref,
+    ids_ref,
+    gates_ref,
+    cache_hbm,
+    out_w_hbm,
+    gate_hbm,
+    up_hbm,
+    down_hbm,
+    out_ref,
+    cache_v,
+    out_w,
+    w_gate,
+    w_up,
+    w_down,
+    q_rows,
+    o_rows,
+    heads_out,
+    heads,
+    part_out,
+    part_in,
+    own_part,
+    hidden,
+    sq_out,
+    sq_in,
+    route,
+    normed,
+    activated,
+    pair_keep,
+    pair_out,
+    pair_in,
+    side_keep,
+    side_out,
+    side_in,
+    line_out,
+    line_in,
+    load_sem,
+    route_s,
+    route_r,
+    head_s,
+    head_r,
+    part_s,
+    part_r,
+    sq_s,
+    sq_r,
+    line_s,
+    line_r,
+    core_s,
+    core_r,
+    side_s,
+    side_r,
+    fwd_s,
+    fwd_r,
+    pair_s,
+    pair_r,
+    back_s,
+    back_r,
+    ret_s,
+    ret_r,
+):
+    f32, bf16 = jnp.float32, jnp.bfloat16
+    ep = lax.axis_index("ep")
+    tp = lax.axis_index("tp")
+    core = lax.rem(ep, CORES)
+    line = lax.div(ep, CORES)
+    chips = ep_size // CORES
+    other_core = ep + 1 - 2 * core
+    other_tp = 1 - tp
+    rows_att = q_ref.shape[0]
+    rows = resid_ref.shape[0]
+    half = resid_ref.shape[1]
+    width = 2 * half
+    hd = new_ref.shape[2] // 2
+    n_heads = q_ref.shape[1] // hd
+    group = n_heads // kvh
+    ctx = cache_v.shape[1] // kvh
+    experts = route.shape[1]
+    half_heads = n_heads // 2
+    half_in = half_heads * hd
+    hidden_units = w_down.shape[0]
+
+    loads = [
+        pltpu.make_async_copy(src, dst, load_sem.at[i])
+        for i, (src, dst) in enumerate(
+            (
+                (cache_hbm, cache_v),
+                (out_w_hbm, out_w),
+                (gate_hbm, w_gate),
+                (up_hbm, w_up),
+                (down_hbm, w_down),
+            )
+        )
+    ]
+    for load in loads:
+        load.start()
+
+    barrier = pltpu.get_barrier_semaphore()
+    for step in range(1, ep_size):
+        pl.semaphore_signal(
+            barrier,
+            inc=1,
+            device_id={"ep": lax.rem(ep + step, ep_size)},
+            device_id_type=MESH,
+        )
+    pl.semaphore_signal(barrier, inc=1, device_id={"tp": other_tp}, device_id_type=MESH)
+
+    def push(src, dst, send, recv, target):
+        return pltpu.make_async_remote_copy(
+            src_ref=src,
+            dst_ref=dst,
+            send_sem=send,
+            recv_sem=recv,
+            device_id=target,
+            device_id_type=MESH,
+        )
+
+    sent = []
+
+    gates = gates_ref[...]
+    shares = gates / jnp.sum(gates, 1, keepdims=True)
+    ids = ids_ref[...]
+    lane = lax.broadcasted_iota(jnp.int32, (rows, 128), 1)
+    dense = jnp.zeros((rows, 128), f32)
+    for k in range(TOPK):
+        dense = dense + jnp.where(ids[:, k : k + 1] == lane, shares[:, k : k + 1], 0.0)
+    if rows < 128:
+        dense = jnp.concatenate([dense, jnp.zeros((128 - rows, 128), f32)], 0)
+    route[ep] = jnp.transpose(dense)[:experts]
+
+    for h in range(0, n_heads, 8):
+        by_head = jnp.stack([q_ref[:, i * hd : (i + 1) * hd].astype(f32) for i in range(h, h + 8)])
+        q_rows[:, h : h + 8, :] = jnp.transpose(by_head, (1, 0, 2))
+
+    scale = 1.0 / math.sqrt(hd)
+    loads[0].wait()
+    span = kvh * ctx
+    head_id = lax.broadcasted_iota(jnp.int32, (n_heads, span), 0)
+    slot_id = lax.broadcasted_iota(jnp.int32, (n_heads, span), 1)
+    same_group = (head_id // group) == (slot_id // ctx)
+    position = jnp.where(same_group, slot_id % ctx, ctx)
+
+    def attend_row(r):
+        q_f = q_rows[r]
+        kv = cache_v[r]
+        scores = (
+            lax.dot_general(
+                q_f.astype(bf16),
+                kv[:, :hd],
+                (((1,), (1,)), ((), ())),
+                preferred_element_type=f32,
+            )
+            * scale
+        )
+        fresh_kv = new_ref[r].astype(f32)
+        fresh_kv = jnp.broadcast_to(fresh_kv[:, None, :], (kvh, group, 2 * hd)).reshape(
+            n_heads, 2 * hd
+        )
+        fresh = jnp.sum(q_f * fresh_kv[:, :hd], 1, keepdims=True) * scale
+        valid = position < len_ref[r]
+        masked = jnp.where(valid, scores, -1e30)
+        top = jnp.maximum(jnp.max(masked, 1, keepdims=True), fresh)
+        terms = jnp.where(valid, jnp.exp(masked - top), 0.0)
+        fresh_term = jnp.exp(fresh - top)
+        total = jnp.sum(terms, 1, keepdims=True) + fresh_term
+        weights = (terms / total).astype(bf16)
+        fresh_weight = (fresh_term / total).astype(bf16).astype(f32)
+        mixed = jnp.dot(weights, kv[:, hd:], preferred_element_type=f32)
+        mixed = mixed + fresh_weight * fresh_kv[:, hd:]
+        o_rows[r] = mixed
+
+    for r in range(rows_att):
+        attend_row(r)
+
+    pl.semaphore_wait(barrier, ep_size)
+
+    def place_heads(owner, dst, at):
+        for i in range(0, half_heads, 8):
+            start = pl.multiple_of(owner * half_heads + i, 8)
+            by_head = jnp.transpose(o_rows[:, pl.ds(start, 8), :], (1, 0, 2)).astype(bf16)
+            for j in range(8):
+                dst[at, (i + j) * hd : (i + j + 1) * hd] = by_head[j]
+
+    place_heads(other_tp, heads_out, slice(None))
+    my_rows = pl.ds(pl.multiple_of(tp * rows_att, rows_att), rows_att)
+    head_copy = push(heads_out, heads.at[my_rows, :], head_s, head_r, {"tp": other_tp})
+    head_copy.start()
+    place_heads(tp, heads, my_rows)
+
+    route_copies = []
+    for step in range(1, ep_size):
+        copy = push(
+            route.at[ep],
+            route.at[ep],
+            route_s.at[step],
+            route_r.at[step],
+            {"ep": lax.rem(ep + step, ep_size)},
+        )
+        copy.start()
+        route_copies.append(copy)
+
+    loads[1].wait()
+    head_copy.wait()
+
+    chunks = part_out.shape[0]
+    chunk = half // chunks
+    part_copies = []
+    for i in range(chunks):
+        def project(j, carry, i=i):
+            at = pl.multiple_of(j * TILE, TILE)
+            cols = pl.ds(pl.multiple_of(other_tp * half + i * chunk + at, TILE), TILE)
+            part_out[i, :, pl.ds(at, TILE)] = jnp.dot(
+                heads[...], out_w[:, cols], preferred_element_type=f32
+            ).astype(bf16)
+            return carry
+
+        lax.fori_loop(0, chunk // TILE, project, 0)
+        copy = push(
+            part_out.at[i], part_in.at[i], part_s.at[i], part_r.at[i], {"tp": other_tp}
+        )
+        copy.start()
+        part_copies.append(copy)
+
+    def project_own(j, carry):
+        at = pl.multiple_of(j * TILE, TILE)
+        cols = pl.ds(pl.multiple_of(tp * half + at, TILE), TILE)
+        own_part[:, pl.ds(at, TILE)] = jnp.dot(
+            heads[...], out_w[:, cols], preferred_element_type=f32
+        ) + resid_ref[:, pl.ds(at, TILE)].astype(f32)
+        return carry
+
+    lax.fori_loop(0, half // TILE, project_own, 0)
+
+    squares = jnp.zeros((rows, 1), f32)
+    for i in range(chunks):
+        part_copies[i].wait()
+        cols = slice(i * chunk, (i + 1) * chunk)
+        total = (own_part[:, cols] + part_in[i].astype(f32)).astype(bf16)
+        hidden[:, cols] = total
+        total = total.astype(f32)
+        squares = squares + jnp.sum(total * total, 1, keepdims=True)
+    sq_out[...] = jnp.broadcast_to(squares, sq_out.shape)
+    sq_copy = push(sq_out, sq_in, sq_s, sq_r, {"tp": other_tp})
+    sq_copy.start()
+    my_cols = pl.ds(pl.multiple_of(tp * half, half), half)
+    their_cols = pl.ds(pl.multiple_of(other_tp * half, half), half)
+    gain = gain_ref[:, my_cols]
+    sq_copy.wait()
+    inv = lax.rsqrt((squares + sq_in[:, :1]) / width + epsilon)
+
+    def block(chip, which, cols):
+        return normed.at[pl.ds(pl.multiple_of((chip * CORES + which) * rows, rows), rows), cols]
+
+    own_block = block(line, core, my_cols)
+    own_block[...] = (hidden[...].astype(f32) * inv * gain).astype(bf16)
+
+    lines = [None]
+    for step in range(1, chips):
+        copy = push(
+            own_block,
+            own_block,
+            line_s.at[step],
+            line_r.at[step],
+            {"ep": lax.rem(line + step, chips) * CORES + core},
+        )
+        copy.start()
+        lines.append(copy)
+    sources = [lax.rem(line + chips - step, chips) for step in range(chips)]
+    cores, sides, forwards = {}, {}, {}
+
+    def spread(k):
+        if k > 0:
+            lines[k].wait_recv()
+        here = block(sources[k], core, my_cols)
+        sides[k] = push(here, here, side_s.at[k], side_r.at[k], {"tp": other_tp})
+        sides[k].start()
+        cores[k] = push(here, here, core_s.at[k], core_r.at[k], {"ep": other_core})
+        cores[k].start()
+
+    def forward(k):
+        sides[k].wait_recv()
+        there = block(sources[k], core, their_cols)
+        forwards[k] = push(there, there, fwd_s.at[k], fwd_r.at[k], {"ep": other_core})
+        forwards[k].start()
+
+    pairs, backs, rets = {}, {}, {}
+    expert = CORES * ep + tp
+
+    def column(owner):
+        row = route[owner, pl.ds(expert, 1), :]
+        return jnp.transpose(jnp.broadcast_to(row, (128, 128)))[:rows, :1]
+
+    def feed(k):
+        cores[k].wait_recv()
+        forwards[k].wait_recv()
+        first = pl.multiple_of(sources[k] * (CORES * rows), CORES * rows)
+        both = pl.ds(first, CORES * rows)
+
+        def up_tile(j, carry):
+            cols = pl.ds(pl.multiple_of(j * TILE, TILE), TILE)
+            values = normed[both, :]
+            gate_proj = jnp.dot(values, w_gate[:, cols], preferred_element_type=f32)
+            up_proj = jnp.dot(values, w_up[:, cols], preferred_element_type=f32)
+            silu = gate_proj / (1.0 + jnp.exp(-gate_proj))
+            activated[:, cols] = (silu * up_proj).astype(bf16)
+            return carry
+
+        lax.fori_loop(0, hidden_units // TILE, up_tile, 0)
+        kept = pl.ds(pl.multiple_of(core * rows, rows), rows)
+        given = pl.ds(pl.multiple_of((1 - core) * rows, rows), rows)
+        keep_weight = column(sources[k] * CORES + core)
+        give_weight = column(sources[k] * CORES + 1 - core)
+
+        def down_tile(j, carry):
+            cols = pl.ds(pl.multiple_of(j * TILE, TILE), TILE)
+            pair_out[k, :, cols] = (
+                jnp.dot(activated[given, :], w_down[:, cols], preferred_element_type=f32)
+                * give_weight
+            ).astype(bf16)
+            pair_keep[k, :, cols] = (
+                jnp.dot(activated[kept, :], w_down[:, cols], preferred_element_type=f32)
+                * keep_weight
+            )
+            return carry
+
+        lax.fori_loop(0, width // TILE, down_tile, 0)
+        pairs[k] = push(
+            pair_out.at[k], pair_in.at[k], pair_s.at[k], pair_r.at[k], {"ep": other_core}
+        )
+        pairs[k].start()
+
+    def cross(k):
+        pairs[k].wait_recv()
+        side_out[k] = (
+            pair_keep[k, :, their_cols] + pair_in[k, :, their_cols].astype(f32)
+        ).astype(bf16)
+        backs[k] = push(
+            side_out.at[k], side_in.at[k], back_s.at[k], back_r.at[k], {"tp": other_tp}
+        )
+        backs[k].start()
+        side_keep[k] = pair_keep[k, :, my_cols] + pair_in[k, :, my_cols].astype(f32)
+
+    def give_back(k):
+        backs[k].wait_recv()
+        total = side_keep[k] + side_in[k].astype(f32)
+        if k == 0:
+            side_keep[k] = total + hidden[...].astype(f32)
+            return
+        line_out[k] = total.astype(bf16)
+        rets[k] = push(
+            line_out.at[k],
+            line_in.at[k],
+            ret_s.at[k],
+            ret_r.at[k],
+            {"ep": sources[k] * CORES + core},
+        )
+        rets[k].start()
+
+    spread(0)
+    for copy in route_copies:
+        copy.wait()
+    for load in loads[2:]:
+        load.wait()
+    forward(0)
+    for k in range(chips):
+        if k + 1 < chips:
+            spread(k + 1)
+        feed(k)
+        if k + 1 < chips:
+            forward(k + 1)
+        if k > 0:
+            give_back(k - 1)
+        cross(k)
+    give_back(chips - 1)
+    result = side_keep[0]
+    for k in range(1, chips):
+        rets[k].wait_recv()
+        result = result + line_in[k].astype(f32)
+    out_ref[...] = result.astype(bf16)
+    for k in range(chips):
+        cores[k].wait_send()
+        sides[k].wait_send()
+        forwards[k].wait_send()
+        pairs[k].wait_send()
+        backs[k].wait_send()
+        if k > 0:
+            lines[k].wait_send()
+            rets[k].wait_send()
+
+
+def fused(
+    queries,
+    new_kv,
+    cache,
+    lengths,
+    out_weight,
+    residual,
+    norm_gain,
+    expert_ids,
+    expert_gates,
+    w_gate,
+    w_up,
+    w_down,
+):
+    f32, bf16 = jnp.float32, jnp.bfloat16
+    ep_size = lax.axis_size("ep")
+    chips = ep_size // CORES
+    rows_att, in_width = queries.shape
+    kvh, ctx, kv_width = cache.shape[1:]
+    hd = kv_width // 2
+    group = in_width // (hd * kvh)
+    rows, half = residual.shape
+    width = 2 * half
+    experts = ep_size * EXP_DEV
+    chunks = 2
+    vmem = pl.BlockSpec(memory_space=pltpu.VMEM)
+    hbm = pl.BlockSpec(memory_space=pl.ANY)
+    smem = pl.BlockSpec(memory_space=pltpu.SMEM)
+    V = pltpu.VMEM
+    dma = pltpu.SemaphoreType.DMA
+    scratch = [
+        V((rows_att, kvh * ctx, kv_width), bf16),
+        V(out_weight.shape, bf16),
+        V(w_gate.shape, bf16),
+        V(w_up.shape, bf16),
+        V(w_down.shape, bf16),
+        V((rows_att, in_width // hd, hd), f32),
+        V((rows_att, in_width // hd, hd), f32),
+        V((rows_att, in_width // 2), bf16),
+        V((rows, in_width // 2), bf16),
+        V((chunks, rows, half // chunks), bf16),
+        V((chunks, rows, half // chunks), bf16),
+        V((rows, half), f32),
+        V((rows, half), bf16),
+        V((rows, 128), f32),
+        V((rows, 128), f32),
+        V((ep_size, experts, 128), f32),
+        V((ep_size * rows, width), bf16),
+        V((CORES * rows, w_down.shape[0]), bf16),
+        V((chips, rows, width), f32),
+        V((chips, rows, width), bf16),
+        V((chips, rows, width), bf16),
+        V((chips, rows, half), f32),
+        V((chips, rows, half), bf16),
+        V((chips, rows, half), bf16),
+        V((chips, rows, half), bf16),
+        V((chips, rows, half), bf16),
+        dma((5,)),
+        dma((ep_size,)),
+        dma((ep_size,)),
+        dma,
+        dma,
+        dma((chunks,)),
+        dma((chunks,)),
+        dma,
+        dma,
+    ] + [dma((chips,)) for _ in range(14)]
+    return pl.pallas_call(
+        functools.partial(layer_kernel, ep_size, kvh),
+        out_shape=jax.ShapeDtypeStruct((rows, half), bf16),
+        in_specs=[vmem, vmem, smem, vmem, vmem, vmem, vmem, hbm, hbm, hbm, hbm, hbm],
+        out_specs=vmem,
+        scratch_shapes=scratch,
+        compiler_params=pltpu.CompilerParams(
+            collective_id=0, has_side_effects=True, vmem_limit_bytes=56 * 1024 * 1024
+        ),
+    )(
+        queries,
+        new_kv,
+        lengths,
+        residual,
+        norm_gain.reshape(1, width),
+        expert_ids,
+        expert_gates,
+        cache.reshape(rows_att, kvh * ctx, kv_width),
+        out_weight,
+        w_gate,
+        w_up,
+        w_down,
+    )
+
+
 def solution(mesh):
     in_specs = (
         P(("groups", "ep", "tp"), None),
@@ -151,6 +645,7 @@
         P(("ep", "tp"), None),
     )
     out_specs = P(("groups", "ep"), "tp")
+    body = fused if mesh.shape["tp"] == EXP_DEV else per_device
     return jax.shard_map(
-        per_device, mesh=mesh, in_specs=in_specs, out_specs=out_specs, check_vma=False
+        body, mesh=mesh, in_specs=in_specs, out_specs=out_specs, check_vma=False
     )

time: 211 us -> 75.8 us (0.36)
  blocking collectives: 73.5 us -> 0 us
  Pallas kernels: 0 us -> 71.3 us
  waiting for transfers between devices: 68.8 us -> 0 us
  matrix products: 21.2 us -> 0 us
  other arithmetic: 13.6 us -> 0 us
  between operations: 13.6 us -> 0.01 us
  local copies, waits for them, and re-layouts: 15.7 us -> 4.32 us
  starting transfers between devices: 4.56 us -> 0 us
    pallas_call x0 -> x1, Pallas kernels: none -> 71.3 us  [fused(): pl.pallas_call(functools.partial(layer_kernel, ep_size, kvh), out_shape=j...]
    all_to_all x2 -> x0, blocking collectives: 62.9 us -> none  [the longest x1 53.7 us: per_device(): lax.all_to_all(outgoing, 'ep', split_axis=0, concat_axis=0, tiled=True)]
    all_to_all x1 -> x0, waiting for transfers between devices: 44.4 us -> none  [run_expert(): lax.all_to_all(projected.astype(jnp.bfloat16), 'ep', split_axis=0, concat...]
    reduce_scatter x2 -> x0, waiting for transfers between devices: 24.5 us -> none  [the longest x1 14.7 us: per_device(): lax.psum_scatter(partial_value, 'tp', scatter_dimension=1, tiled=True)]
    dot_general x7 -> x0, matrix products: 21.2 us -> none  [the longest x1 8.28 us: run_expert(): jnp.einsum('qcf,fd->qcd', activated, w_down, preferred_element_type=jnp.f...]
    gather x6 -> x0, local copies, waits for them, and re-layouts: 11.7 us -> none  [the longest x1 7.61 us: per_device(): moe_part = jnp.sum(weight[:, :, None] * flat[index], 1)]
    reduce_sum x4 -> x0, other arithmetic: 5.9 us -> none  [the longest x1 4.35 us: per_device(): moe_part = jnp.sum(weight[:, :, None] * flat[index], 1)]
    all_gather x1 -> x0, blocking collectives: 5.64 us -> none  [per_device(): normed_full = lax.all_gather(normed_share, 'tp', axis=1, tiled=True)]
  transfers between devices with their start and end apart: 3 -> 0, of which waited for: 3 -> 0; matrix products, arithmetic and copies ran while one was open for 2% -> 0% of each run, Pallas kernels for 0% -> 0%
where the time goes in v1:
time: 75.8 us; the launch traced here: 75.6 us
  Pallas kernels  71.3 us (94%)
  local copies, waits for them, and re-layouts  4.32 us (6%)
    pallas_call x1, Pallas kernels, fused(): pl.pallas_call(functools.partial(layer_kernel, ep_size, kvh), out_shape=j...  71.3 us
    unnamed x3, local copies, waits for them, and re-layouts  4.32 us

profile of v1, /device:TPU:0, one launch (start us, length us, event | category | flops | bytes accessed | tf_op | source)
XLA Modules:
  0.0 75.6 jit_solution(7323478450165829723)
XLA Ops:
  0.0 1.4 %copy.13.ids_ref = s32[64,8]{1,0:T(8,128)} copy(s32[64,8]{0,1:T(8,128)} %param.19) | data formatting | bytes 4096 | tf_op args[7]
  1.4 1.4 %copy.14.gates_ref = f32[64,8]{1,0:T(8,128)} copy(f32[64,8]{0,1:T(8,128)} %param.20) | data formatting | bytes 4096 | tf_op args[8]
  2.8 71.3 %shard_map.118 = bf16[64,1024]{1,0:T(8,128)(2,1)} custom-call(bf16[32,4096]{1,0:T(8,128)(2,1)} %q_ref.1, bf16[32,4,256]{2,1,0:T(4,128)(2,1)} %new_ref.1, s32[32]{0:T(128)} %len_ref.1, bf16[64,1024]{1,0:T(8,128)(2,1)} %resid_ref.1, f32[1,2048]{1,0:T(1,128)} %bitcast.3, s32[64,8]{1,0:T(8,128)} %copy.13.ids_ref, f32[64,8]{1,0:T(8,128)} %copy.14.gates_ref, ...), custom_call_target="tpu_custom_call" | custom-call | tf_op jit(solution)/shard_map/pallas_call | solution.py:607
  74.0 1.6 %copy.16 = bf16[64,1024]{1,0:T(8,128)(2,1)} copy(bf16[64,1024]{1,0:T(8,128)(2,1)} %shard_map.118) | data formatting | bytes 262144

commit v2 on v1

--- a/solution.py
+++ b/solution.py
@@ -11,6 +11,7 @@
 MESH = pl.DeviceIdType.MESH
 CORES = 2
 TILE = 256
+BATCH = 4
 
 D = 2048
 TOPK = 8
@@ -267,15 +268,15 @@
     sent = []
 
     gates = gates_ref[...]
-    shares = gates / jnp.sum(gates, 1, keepdims=True)
+    shares = gates / jnp.sum(gates, 0, keepdims=True)
     ids = ids_ref[...]
-    lane = lax.broadcasted_iota(jnp.int32, (rows, 128), 1)
-    dense = jnp.zeros((rows, 128), f32)
+    expert_id = lax.broadcasted_iota(jnp.int32, (experts, rows), 0)
+    dense = jnp.zeros((experts, rows), f32)
     for k in range(TOPK):
-        dense = dense + jnp.where(ids[:, k : k + 1] == lane, shares[:, k : k + 1], 0.0)
+        dense = dense + jnp.where(ids[k : k + 1] == expert_id, shares[k : k + 1], 0.0)
     if rows < 128:
-        dense = jnp.concatenate([dense, jnp.zeros((128 - rows, 128), f32)], 0)
-    route[ep] = jnp.transpose(dense)[:experts]
+        dense = jnp.concatenate([dense, jnp.zeros((experts, 128 - rows), f32)], 1)
+    route[ep] = dense
 
     for h in range(0, n_heads, 8):
         by_head = jnp.stack([q_ref[:, i * hd : (i + 1) * hd].astype(f32) for i in range(h, h + 8)])
@@ -284,29 +285,43 @@
     scale = 1.0 / math.sqrt(hd)
     loads[0].wait()
     span = kvh * ctx
+    tall = BATCH * n_heads
     head_id = lax.broadcasted_iota(jnp.int32, (n_heads, span), 0)
     slot_id = lax.broadcasted_iota(jnp.int32, (n_heads, span), 1)
     same_group = (head_id // group) == (slot_id // ctx)
     position = jnp.where(same_group, slot_id % ctx, ctx)
 
-    def attend_row(r):
-        q_f = q_rows[r]
-        kv = cache_v[r]
-        scores = (
-            lax.dot_general(
-                q_f.astype(bf16),
-                kv[:, :hd],
-                (((1,), (1,)), ((), ())),
-                preferred_element_type=f32,
-            )
-            * scale
-        )
-        fresh_kv = new_ref[r].astype(f32)
-        fresh_kv = jnp.broadcast_to(fresh_kv[:, None, :], (kvh, group, 2 * hd)).reshape(
-            n_heads, 2 * hd
+    def attend_rows(first):
+        q_f = q_rows[first : first + BATCH].reshape(tall, hd)
+        q_b = q_f.astype(bf16)
+        each = range(BATCH)
+        kv = [cache_v[first + i] for i in each]
+        scores = jnp.concatenate(
+            [
+                lax.dot_general(
+                    q_b[i * n_heads : (i + 1) * n_heads],
+                    kv[i][:, :hd],
+                    (((1,), (1,)), ((), ())),
+                    preferred_element_type=f32,
+                )
+                for i in each
+            ],
+            0,
+        )
+        scores = scores * scale
+        fresh_kv = jnp.concatenate(
+            [
+                jnp.broadcast_to(
+                    new_ref[first + i].astype(f32)[:, None, :], (kvh, group, 2 * hd)
+                ).reshape(n_heads, 2 * hd)
+                for i in each
+            ],
+            0,
         )
         fresh = jnp.sum(q_f * fresh_kv[:, :hd], 1, keepdims=True) * scale
-        valid = position < len_ref[r]
+        valid = jnp.concatenate(
+            [jnp.where(position < len_ref[first + i], 1.0, 0.0) for i in each], 0
+        ) > 0.5
         masked = jnp.where(valid, scores, -1e30)
         top = jnp.maximum(jnp.max(masked, 1, keepdims=True), fresh)
         terms = jnp.where(valid, jnp.exp(masked - top), 0.0)
@@ -314,27 +329,45 @@
         total = jnp.sum(terms, 1, keepdims=True) + fresh_term
         weights = (terms / total).astype(bf16)
         fresh_weight = (fresh_term / total).astype(bf16).astype(f32)
-        mixed = jnp.dot(weights, kv[:, hd:], preferred_element_type=f32)
+        mixed = jnp.concatenate(
+            [
+                jnp.dot(
+                    weights[i * n_heads : (i + 1) * n_heads],
+                    kv[i][:, hd:],
+                    preferred_element_type=f32,
+                )
+                for i in each
+            ],
+            0,
+        )
         mixed = mixed + fresh_weight * fresh_kv[:, hd:]
-        o_rows[r] = mixed
-
-    for r in range(rows_att):
-        attend_row(r)
-
-    pl.semaphore_wait(barrier, ep_size)
-
-    def place_heads(owner, dst, at):
+        o_rows[first : first + BATCH] = mixed.reshape(BATCH, n_heads, hd)
+
+    part = rows_att // 2
+
+    def place_heads(owner, first, dst, at):
         for i in range(0, half_heads, 8):
             start = pl.multiple_of(owner * half_heads + i, 8)
-            by_head = jnp.transpose(o_rows[:, pl.ds(start, 8), :], (1, 0, 2)).astype(bf16)
+            by_head = jnp.transpose(o_rows[first : first + part, pl.ds(start, 8), :], (1, 0, 2))
+            by_head = by_head.astype(bf16)
             for j in range(8):
                 dst[at, (i + j) * hd : (i + j + 1) * hd] = by_head[j]
 
-    place_heads(other_tp, heads_out, slice(None))
-    my_rows = pl.ds(pl.multiple_of(tp * rows_att, rows_att), rows_att)
-    head_copy = push(heads_out, heads.at[my_rows, :], head_s, head_r, {"tp": other_tp})
-    head_copy.start()
-    place_heads(tp, heads, my_rows)
+    head_copies = []
+    for p in range(2):
+        for first in range(p * part, (p + 1) * part, BATCH):
+            attend_rows(first)
+        if p == 0:
+            pl.semaphore_wait(barrier, ep_size)
+        here = pl.ds(p * part, part)
+        there = pl.ds(pl.multiple_of(tp * rows_att + p * part, part), part)
+        place_heads(other_tp, p * part, heads_out, here)
+        copy = push(
+            heads_out.at[here, :], heads.at[there, :], head_s.at[p], head_r.at[p], {"tp": other_tp}
+        )
+        copy.start()
+        head_copies.append(copy)
+        place_heads(tp, p * part, heads, there)
 
     route_copies = []
     for step in range(1, ep_size):
@@ -349,7 +382,8 @@
         route_copies.append(copy)
 
     loads[1].wait()
-    head_copy.wait()
+    for copy in head_copies:
+        copy.wait()
 
     chunks = part_out.shape[0]
     chunk = half // chunks
@@ -439,6 +473,9 @@
         row = route[owner, pl.ds(expert, 1), :]
         return jnp.transpose(jnp.broadcast_to(row, (128, 128)))[:rows, :1]
 
+    low = pl.ds(pl.multiple_of((1 - core) * rows, rows), rows)
+    high = pl.ds(pl.multiple_of(core * rows, rows), rows)
+
     def feed(k):
         cores[k].wait_recv()
         forwards[k].wait_recv()
@@ -451,43 +488,43 @@
             gate_proj = jnp.dot(values, w_gate[:, cols], preferred_element_type=f32)
             up_proj = jnp.dot(values, w_up[:, cols], preferred_element_type=f32)
             silu = gate_proj / (1.0 + jnp.exp(-gate_proj))
-            activated[:, cols] = (silu * up_proj).astype(bf16)
+            both_rows = (silu * up_proj).astype(bf16)
+            activated[low, cols] = both_rows[:rows]
+            activated[high, cols] = both_rows[rows:]
             return carry
 
         lax.fori_loop(0, hidden_units // TILE, up_tile, 0)
-        kept = pl.ds(pl.multiple_of(core * rows, rows), rows)
-        given = pl.ds(pl.multiple_of((1 - core) * rows, rows), rows)
         keep_weight = column(sources[k] * CORES + core)
         give_weight = column(sources[k] * CORES + 1 - core)
 
-        def down_tile(j, carry):
-            cols = pl.ds(pl.multiple_of(j * TILE, TILE), TILE)
-            pair_out[k, :, cols] = (
-                jnp.dot(activated[given, :], w_down[:, cols], preferred_element_type=f32)
-                * give_weight
-            ).astype(bf16)
-            pair_keep[k, :, cols] = (
-                jnp.dot(activated[kept, :], w_down[:, cols], preferred_element_type=f32)
-                * keep_weight
+        for h, owner in enumerate((other_tp, tp)):
+            def down_tile(j, carry, h=h, owner=owner):
+                at = pl.multiple_of(j * TILE, TILE)
+                cols = pl.ds(pl.multiple_of(owner * half + at, TILE), TILE)
+                value = jnp.dot(activated[...], w_down[:, cols], preferred_element_type=f32)
+                pair_out[k, h, :, pl.ds(at, TILE)] = (value[:rows] * give_weight).astype(bf16)
+                pair_keep[k, h, :, pl.ds(at, TILE)] = value[rows:] * keep_weight
+                return carry
+
+            lax.fori_loop(0, half // TILE, down_tile, 0)
+            pairs[k, h] = push(
+                pair_out.at[k, h],
+                pair_in.at[k, h],
+                pair_s.at[k, h],
+                pair_r.at[k, h],
+                {"ep": other_core},
             )
-            return carry
-
-        lax.fori_loop(0, width // TILE, down_tile, 0)
-        pairs[k] = push(
-            pair_out.at[k], pair_in.at[k], pair_s.at[k], pair_r.at[k], {"ep": other_core}
-        )
-        pairs[k].start()
+            pairs[k, h].start()
 
     def cross(k):
-        pairs[k].wait_recv()
-        side_out[k] = (
-            pair_keep[k, :, their_cols] + pair_in[k, :, their_cols].astype(f32)
-        ).astype(bf16)
+        pairs[k, 0].wait_recv()
+        side_out[k] = (pair_keep[k, 0] + pair_in[k, 0].astype(f32)).astype(bf16)
         backs[k] = push(
             side_out.at[k], side_in.at[k], back_s.at[k], back_r.at[k], {"tp": other_tp}
         )
         backs[k].start()
-        side_keep[k] = pair_keep[k, :, my_cols] + pair_in[k, :, my_cols].astype(f32)
+        pairs[k, 1].wait_recv()
+        side_keep[k] = pair_keep[k, 1] + pair_in[k, 1].astype(f32)
 
     def give_back(k):
         backs[k].wait_recv()
@@ -530,7 +567,8 @@
         cores[k].wait_send()
         sides[k].wait_send()
         forwards[k].wait_send()
-        pairs[k].wait_send()
+        pairs[k, 0].wait_send()
+        pairs[k, 1].wait_send()
         backs[k].wait_send()
         if k > 0:
             lines[k].wait_send()
@@ -586,9 +624,9 @@
         V((ep_size, experts, 128), f32),
         V((ep_size * rows, width), bf16),
         V((CORES * rows, w_down.shape[0]), bf16),
-        V((chips, rows, width), f32),
-        V((chips, rows, width), bf16),
-        V((chips, rows, width), bf16),
+        V((chips, 2, rows, half), f32),
+        V((chips, 2, rows, half), bf16),
+        V((chips, 2, rows, half), bf16),
         V((chips, rows, half), f32),
         V((chips, rows, half), bf16),
         V((chips, rows, half), bf16),
@@ -597,13 +635,13 @@
         dma((5,)),
         dma((ep_size,)),
         dma((ep_size,)),
-        dma,
-        dma,
+        dma((2,)),
+        dma((2,)),
         dma((chunks,)),
         dma((chunks,)),
         dma,
         dma,
-    ] + [dma((chips,)) for _ in range(14)]
+    ] + [dma((chips,)) for _ in range(8)] + [dma((chips, 2))] * 2 + [dma((chips,)) for _ in range(4)]
     return pl.pallas_call(
         functools.partial(layer_kernel, ep_size, kvh),
         out_shape=jax.ShapeDtypeStruct((rows, half), bf16),
@@ -619,8 +657,8 @@
         lengths,
         residual,
         norm_gain.reshape(1, width),
-        expert_ids,
-        expert_gates,
+        expert_ids.T,
+        expert_gates.T,
         cache.reshape(rows_att, kvh * ctx, kv_width),
         out_weight,
         w_gate,

time: 75.8 us -> 63.5 us (0.84)
  Pallas kernels: 71.3 us -> 61.8 us
  local copies, waits for them, and re-layouts: 4.32 us -> 1.57 us
    pallas_call x1, Pallas kernels: 71.3 us -> 61.8 us  [fused(): pl.pallas_call(functools.partial(layer_kernel, ep_size, kvh), out_shape=j...]
    unnamed x3 -> x1, local copies, waits for them, and re-layouts: 4.32 us -> 1.57 us
where the time goes in v2:
time: 63.5 us; the launch traced here: 63.4 us
  Pallas kernels  61.8 us (97%)
  local copies, waits for them, and re-layouts  1.57 us (2%)
    pallas_call x1, Pallas kernels, fused(): pl.pallas_call(functools.partial(layer_kernel, ep_size, kvh), out_shape=j...  61.8 us
    unnamed x1, local copies, waits for them, and re-layouts  1.57 us

profile of v2, /device:TPU:0, one launch (start us, length us, event | category | flops | bytes accessed | tf_op | source)
XLA Modules:
  0.0 63.4 jit_solution(4818809379837138269)
XLA Ops:
  0.0 61.8 %shard_map.118 = bf16[64,1024]{1,0:T(8,128)(2,1)} custom-call(bf16[32,4096]{1,0:T(8,128)(2,1)} %q_ref.1, bf16[32,4,256]{2,1,0:T(4,128)(2,1)} %new_ref.1, s32[32]{0:T(128)} %len_ref.1, bf16[64,1024]{1,0:T(8,128)(2,1)} %resid_ref.1, f32[1,2048]{1,0:T(1,128)} %bitcast.5, s32[8,64]{1,0:T(8,128)} %bitcast.6, f32[8,64]{1,0:T(8,128)} %bitcast.7, ...), custom_call_target="tpu_custom_call" | custom-call | tf_op jit(solution)/shard_map/pallas_call | solution.py:645
  61.8 1.6 %copy.14 = bf16[64,1024]{1,0:T(8,128)(2,1)} copy(bf16[64,1024]{1,0:T(8,128)(2,1)} %shard_map.118) | data formatting | bytes 262144

commit v3 on v2

--- a/solution.py
+++ b/solution.py
@@ -174,6 +174,7 @@
     hidden,
     sq_out,
     sq_in,
+    inv_rows,
     route,
     normed,
     activated,
@@ -194,6 +195,8 @@
     part_r,
     sq_s,
     sq_r,
+    inv_s,
+    inv_r,
     line_s,
     line_r,
     core_s,
@@ -422,20 +425,21 @@
         hidden[:, cols] = total
         total = total.astype(f32)
         squares = squares + jnp.sum(total * total, 1, keepdims=True)
-    sq_out[...] = jnp.broadcast_to(squares, sq_out.shape)
+    wide = jnp.broadcast_to(squares, (rows, 128))
+    if rows < 128:
+        wide = jnp.concatenate([wide, jnp.zeros((128 - rows, 128), f32)], 0)
+    sq_out[...] = jnp.transpose(wide)[:8]
     sq_copy = push(sq_out, sq_in, sq_s, sq_r, {"tp": other_tp})
     sq_copy.start()
     my_cols = pl.ds(pl.multiple_of(tp * half, half), half)
     their_cols = pl.ds(pl.multiple_of(other_tp * half, half), half)
     gain = gain_ref[:, my_cols]
-    sq_copy.wait()
-    inv = lax.rsqrt((squares + sq_in[:, :1]) / width + epsilon)
 
     def block(chip, which, cols):
         return normed.at[pl.ds(pl.multiple_of((chip * CORES + which) * rows, rows), rows), cols]
 
     own_block = block(line, core, my_cols)
-    own_block[...] = (hidden[...].astype(f32) * inv * gain).astype(bf16)
+    own_block[...] = (hidden[...].astype(f32) * gain).astype(bf16)
 
     lines = [None]
     for step in range(1, chips):
@@ -469,8 +473,8 @@
     pairs, backs, rets = {}, {}, {}
     expert = CORES * ep + tp
 
-    def column(owner):
-        row = route[owner, pl.ds(expert, 1), :]
+    def column(table, owner, at):
+        row = table[owner, pl.ds(at, 1), :]
         return jnp.transpose(jnp.broadcast_to(row, (128, 128)))[:rows, :1]
 
     low = pl.ds(pl.multiple_of((1 - core) * rows, rows), rows)
@@ -481,12 +485,15 @@
         forwards[k].wait_recv()
         first = pl.multiple_of(sources[k] * (CORES * rows), CORES * rows)
         both = pl.ds(first, CORES * rows)
+        scaling = jnp.concatenate(
+            [column(inv_rows, sources[k] * CORES + i, 0) for i in range(CORES)], 0
+        )
 
         def up_tile(j, carry):
             cols = pl.ds(pl.multiple_of(j * TILE, TILE), TILE)
             values = normed[both, :]
-            gate_proj = jnp.dot(values, w_gate[:, cols], preferred_element_type=f32)
-            up_proj = jnp.dot(values, w_up[:, cols], preferred_element_type=f32)
+            gate_proj = jnp.dot(values, w_gate[:, cols], preferred_element_type=f32) * scaling
+            up_proj = jnp.dot(values, w_up[:, cols], preferred_element_type=f32) * scaling
             silu = gate_proj / (1.0 + jnp.exp(-gate_proj))
             both_rows = (silu * up_proj).astype(bf16)
             activated[low, cols] = both_rows[:rows]
@@ -494,8 +501,8 @@
             return carry
 
         lax.fori_loop(0, hidden_units // TILE, up_tile, 0)
-        keep_weight = column(sources[k] * CORES + core)
-        give_weight = column(sources[k] * CORES + 1 - core)
+        keep_weight = column(route, sources[k] * CORES + core, expert)
+        give_weight = column(route, sources[k] * CORES + 1 - core, expert)
 
         for h, owner in enumerate((other_tp, tp)):
             def down_tile(j, carry, h=h, owner=owner):
@@ -523,6 +530,8 @@
             side_out.at[k], side_in.at[k], back_s.at[k], back_r.at[k], {"tp": other_tp}
         )
         backs[k].start()
+
+    def keep(k):
         pairs[k, 1].wait_recv()
         side_keep[k] = pair_keep[k, 1] + pair_in[k, 1].astype(f32)
 
@@ -543,11 +552,23 @@
         rets[k].start()
 
     spread(0)
+    sq_copy.wait()
+    inv_rows[ep] = lax.rsqrt((sq_out[...] + sq_in[...]) / width + epsilon)
+    for step in range(1, ep_size):
+        copy = push(
+            inv_rows.at[ep],
+            inv_rows.at[ep],
+            inv_s.at[step],
+            inv_r.at[step],
+            {"ep": lax.rem(ep + step, ep_size)},
+        )
+        copy.start()
+        route_copies.append(copy)
+    forward(0)
     for copy in route_copies:
         copy.wait()
     for load in loads[2:]:
         load.wait()
-    forward(0)
     for k in range(chips):
         if k + 1 < chips:
             spread(k + 1)
@@ -555,8 +576,10 @@
         if k + 1 < chips:
             forward(k + 1)
         if k > 0:
+            keep(k - 1)
             give_back(k - 1)
         cross(k)
+    keep(chips - 1)
     give_back(chips - 1)
     result = side_keep[0]
     for k in range(1, chips):
@@ -619,8 +642,9 @@
         V((chunks, rows, half // chunks), bf16),
         V((rows, half), f32),
         V((rows, half), bf16),
-        V((rows, 128), f32),
-        V((rows, 128), f32),
+        V((8, 128), f32),
+        V((8, 128), f32),
+        V((ep_size, 8, 128), f32),
         V((ep_size, experts, 128), f32),
         V((ep_size * rows, width), bf16),
         V((CORES * rows, w_down.shape[0]), bf16),
@@ -641,6 +665,8 @@
         dma((chunks,)),
         dma,
         dma,
+        dma((ep_size,)),
+        dma((ep_size,)),
     ] + [dma((chips,)) for _ in range(8)] + [dma((chips, 2))] * 2 + [dma((chips,)) for _ in range(4)]
     return pl.pallas_call(
         functools.partial(layer_kernel, ep_size, kvh),

time: 63.5 us -> 65 us (1.024)
  Pallas kernels: 61.8 us -> 63.2 us
    pallas_call x1, Pallas kernels: 61.8 us -> 63.2 us  [fused(): pl.pallas_call(functools.partial(layer_kernel, ep_size, kvh), out_shape=j...]
where the time goes in v3:
time: 65 us; the launch traced here: 64.8 us
  Pallas kernels  63.2 us (97%)
  local copies, waits for them, and re-layouts  1.57 us (2%)
    pallas_call x1, Pallas kernels, fused(): pl.pallas_call(functools.partial(layer_kernel, ep_size, kvh), out_shape=j...  63.2 us
    unnamed x1, local copies, waits for them, and re-layouts  1.57 us

profile of v3, /device:TPU:0, one launch (start us, length us, event | category | flops | bytes accessed | tf_op | source)
XLA Modules:
  0.0 64.8 jit_solution(13806862902226146629)
XLA Ops:
  0.0 63.2 %shard_map.118 = bf16[64,1024]{1,0:T(8,128)(2,1)} custom-call(bf16[32,4096]{1,0:T(8,128)(2,1)} %q_ref.1, bf16[32,4,256]{2,1,0:T(4,128)(2,1)} %new_ref.1, s32[32]{0:T(128)} %len_ref.1, bf16[64,1024]{1,0:T(8,128)(2,1)} %resid_ref.1, f32[1,2048]{1,0:T(1,128)} %bitcast.5, s32[8,64]{1,0:T(8,128)} %bitcast.6, f32[8,64]{1,0:T(8,128)} %bitcast.7, ...), custom_call_target="tpu_custom_call" | custom-call | tf_op jit(solution)/shard_map/pallas_call | solution.py:671
  63.2 1.6 %copy.14 = bf16[64,1024]{1,0:T(8,128)(2,1)} copy(bf16[64,1024]{1,0:T(8,128)(2,1)} %shard_map.118) | data formatting | bytes 262144

commit v4 on v2

--- a/solution.py
+++ b/solution.py
@@ -523,6 +523,8 @@
             side_out.at[k], side_in.at[k], back_s.at[k], back_r.at[k], {"tp": other_tp}
         )
         backs[k].start()
+
+    def keep(k):
         pairs[k, 1].wait_recv()
         side_keep[k] = pair_keep[k, 1] + pair_in[k, 1].astype(f32)
 
@@ -555,8 +557,10 @@
         if k + 1 < chips:
             forward(k + 1)
         if k > 0:
+            keep(k - 1)
             give_back(k - 1)
         cross(k)
+    keep(chips - 1)
     give_back(chips - 1)
     result = side_keep[0]
     for k in range(1, chips):

time: 63.5 us -> 63.6 us (level)
  no operation moved by 1% of the time
where the time goes in v4:
time: 63.6 us; the launch traced here: 63.4 us
  Pallas kernels  61.9 us (97%)
  local copies, waits for them, and re-layouts  1.57 us (2%)
    pallas_call x1, Pallas kernels, fused(): pl.pallas_call(functools.partial(layer_kernel, ep_size, kvh), out_shape=j...  61.9 us
    unnamed x1, local copies, waits for them, and re-layouts  1.57 us

profile of v4, /device:TPU:0, one launch (start us, length us, event | category | flops | bytes accessed | tf_op | source)
XLA Modules:
  0.0 63.4 jit_solution(12098795986083991422)
XLA Ops:
  0.0 61.9 %shard_map.118 = bf16[64,1024]{1,0:T(8,128)(2,1)} custom-call(bf16[32,4096]{1,0:T(8,128)(2,1)} %q_ref.1, bf16[32,4,256]{2,1,0:T(4,128)(2,1)} %new_ref.1, s32[32]{0:T(128)} %len_ref.1, bf16[64,1024]{1,0:T(8,128)(2,1)} %resid_ref.1, f32[1,2048]{1,0:T(1,128)} %bitcast.5, s32[8,64]{1,0:T(8,128)} %bitcast.6, f32[8,64]{1,0:T(8,128)} %bitcast.7, ...), custom_call_target="tpu_custom_call" | custom-call | tf_op jit(solution)/shard_map/pallas_call | solution.py:649
  61.9 1.6 %copy.14 = bf16[64,1024]{1,0:T(8,128)(2,1)} copy(bf16[64,1024]{1,0:T(8,128)(2,1)} %shard_map.118) | data formatting | bytes 262144
